TPU v7x, 128 devices: a whole 4x4x4 slice. The times are simulated.
128 devices in a mesh: ty: 16 (over z, x_lo, core), tx: 8 (over x_hi, y).
Axes of the slice: x: 4 (x_hi: 2, x_lo: 2; x = x_hi * 2 + x_lo), y: 4, z: 4, core: 2. Of those that a mesh axis runs over, the one named last changes fastest.
Arguments:
- image: float32 [4096, 4096], P('ty', 'tx'), may hold values from -6 to 6
- noise: float32 [2, 4096, 4096], P(None, 'ty', 'tx'), may hold values from -6 to 6
- offsets: int32 [2, 2], replicated, may hold values from 1 to 7, as said below
- key_mask: int32 [256, 256], P('ty', 'tx'), may hold values 0 or 1
- gains: float32 [2, 4096, 4096], P(None, ('ty', 'tx')), may hold values from -1 to 1
- observed: float32 [2, 4096, 4096], P(None, ('ty', 'tx')), may hold values from -6 to 6
- vis_weight: float32 [4096, 4096], P(('ty', 'tx')), may hold values from 0.05 to 1
- w_embed: bfloat16 [256, 512], replicated, may hold values from -0.375 to 0.375
- w_qkv: bfloat16 [2, 512, 1536], replicated, as said below
- w_proj: bfloat16 [2, 512, 512], replicated, may hold values from -0.25 to 0.25
- w_up: bfloat16 [2, 512, 2048], replicated, may hold values from -0.25 to 0.25
- w_down: bfloat16 [2, 2048, 512], replicated, may hold values from -0.125 to 0.125
- w_unembed: bfloat16 [512, 256], replicated, may hold values from -0.25 to 0.25
- norm_gains: float32 [2, 2, 512], replicated, may hold values from 0.1 to 1.9
Outputs:
- sampled: float32 [4096, 4096], P('ty', 'tx')
Inputs may be any that keep to these rules, and one draw needn't show every extreme that they name: `offsets`: each entry lies in 1 to 7, and some entry equals 7. `w_qkv`: columns ordered by query, key or value, then head, then feature of the head.
All inputs are finite; a program needn't handle non-finite values. No bound on the sum of `key_mask` on one device may be relied on, other than what follows from the above.
Results may differ from a plain program's by a relative error of at most 0.04.
Values may be sent and summed in bfloat16 or wider, within the bound.
A program may use at most 128 MiB of HBM per device.

v0:
```python
import math

import jax
import jax.numpy as jnp
from jax import lax
from jax.sharding import PartitionSpec as P

N = 4096
PATCH = 16
WIN = 8
D = 512
HEADS = 8
STEPS = 2


SIGMAS = (0.8, 0.5, 0.3)
STEP_SIZES = (0.9, 0.7)
EPSILON = 1e-05
HIGHEST = lax.Precision.HIGHEST


def from_behind(shard, axis, by):
    size = lax.axis_size(axis)
    return lax.ppermute(shard, axis, [(i, (i + by) % size) for i in range(size)])


def counting(length):
    return jnp.arange(length, dtype=jnp.int32)


def roots(length, outer, inner, sign):
    product = outer[:, None] * inner[None, :] % length
    angle = 2.0 * math.pi / length * product.astype(jnp.float32)
    return (jnp.cos(angle), sign * jnp.sin(angle))


def complex_einsum(form, left, right):
    real = jnp.einsum(form, left[0], right[0], precision=HIGHEST) - jnp.einsum(
        form, left[1], right[1], precision=HIGHEST
    )
    imag = jnp.einsum(form, left[0], right[1], precision=HIGHEST) + jnp.einsum(
        form, left[1], right[0], precision=HIGHEST
    )
    return (real, imag)


def complex_times(left, right):
    return (left[0] * right[0] - left[1] * right[1], left[0] * right[1] + left[1] * right[0])


def along_last(real_part, imag_part, groups, sign):
    rows, length = real_part.shape
    inner = length // groups
    first = roots(groups, counting(groups), counting(groups), sign)
    twist = roots(length, counting(inner), counting(groups), sign)
    second = roots(inner, counting(inner), counting(inner), sign)
    shaped = real_part.reshape(rows, groups, inner)
    if imag_part is None:
        partial_value = (
            jnp.einsum("mab,ka->mbk", shaped, first[0], precision=HIGHEST),
            jnp.einsum("mab,ka->mbk", shaped, first[1], precision=HIGHEST),
        )
    else:
        partial_value = complex_einsum(
            "mab,ka->mbk", (shaped, imag_part.reshape(rows, groups, inner)), first
        )
    partial_value = complex_times(partial_value, twist)
    result = complex_einsum("jb,mbk->mjk", second, partial_value)
    return (result[0].reshape(rows, length), result[1].reshape(rows, length))


def across_groups(pair, lead, trail, sign, keep_imag):
    rows, cols = pair[0].shape
    inner = rows // lead
    width = cols // trail
    groups = lead * trail
    length = groups * inner
    first = roots(groups, counting(groups), counting(groups), sign)
    first = (first[0].reshape(groups, lead, trail), first[1].reshape(groups, lead, trail))
    twist = roots(length, counting(inner), counting(groups), sign)
    second = roots(inner, counting(inner), counting(inner), sign)
    shaped = (
        pair[0].reshape(lead, inner, trail, width),
        pair[1].reshape(lead, inner, trail, width),
    )
    partial_value = complex_einsum("gbhc,kgh->cbk", shaped, first)
    partial_value = complex_times(partial_value, twist)
    if keep_imag:
        result = complex_einsum("jb,cbk->cjk", second, partial_value)
        return (result[0].reshape(width, length), result[1].reshape(width, length))
    real = jnp.einsum("jb,cbk->cjk", second[0], partial_value[0], precision=HIGHEST) - jnp.einsum(
        "jb,cbk->cjk", second[1], partial_value[1], precision=HIGHEST
    )
    return real.reshape(width, length)


def likelihood(tile, gains, observed, vis_weight):
    devices = lax.axis_size("ty") * lax.axis_size("tx")
    slab = lax.all_to_all(
        tile.astype(jnp.bfloat16), "tx", split_axis=0, concat_axis=1, tiled=True
    ).astype(tile.dtype)
    spec_re, spec_im = along_last(slab, None, devices, -1.0)
    moved = (
        lax.all_to_all(
            spec_re.astype(jnp.bfloat16), ("ty", "tx"), split_axis=1, concat_axis=1, tiled=True
        ).astype(spec_re.dtype),
        lax.all_to_all(
            spec_im.astype(jnp.bfloat16), ("ty", "tx"), split_axis=1, concat_axis=1, tiled=True
        ).astype(spec_im.dtype),
    )
    lead = 1
    spectrum = across_groups(moved, lead, devices // lead, -1.0, True)
    spectrum = (spectrum[0] * (1.0 / N), spectrum[1] * (1.0 / N))
    model = complex_times((gains[0], gains[1]), spectrum)
    misfit = (vis_weight * (model[0] - observed[0]), vis_weight * (model[1] - observed[1]))
    back = complex_times((gains[0], -gains[1]), misfit)
    wave_re, wave_im = along_last(back[0], back[1], devices, 1.0)
    returned = (
        lax.all_to_all(
            wave_re.astype(jnp.bfloat16), ("ty", "tx"), split_axis=1, concat_axis=1, tiled=True
        ).astype(wave_re.dtype),
        lax.all_to_all(
            wave_im.astype(jnp.bfloat16), ("ty", "tx"), split_axis=1, concat_axis=1, tiled=True
        ).astype(wave_im.dtype),
    )
    slab_grad = across_groups(returned, lead, devices // lead, 1.0, False) * (1.0 / N)
    return lax.all_to_all(
        slab_grad.astype(jnp.bfloat16), "tx", split_axis=1, concat_axis=0, tiled=True
    ).astype(slab_grad.dtype)


def layer_norm(values, gain):
    centre = jnp.mean(values, axis=-1, keepdims=True)
    shifted = values - centre
    spread = jnp.mean(shifted * shifted, axis=-1, keepdims=True)
    return shifted * lax.rsqrt(spread + EPSILON) * gain


def to_windows(grid):
    rows, cols, feats = grid.shape
    shaped = grid.reshape(rows // WIN, WIN, cols // WIN, WIN, feats).transpose(0, 2, 1, 3, 4)
    return shaped.reshape(rows // WIN * (cols // WIN), WIN * WIN, feats)


def from_windows(windows, rows, cols):
    feats = windows.shape[-1]
    shaped = windows.reshape(rows // WIN, cols // WIN, WIN, WIN, feats).transpose(0, 2, 1, 3, 4)
    return shaped.reshape(rows, cols, feats)


def attention(normed, labels, keep, w_qkv, w_proj):
    rows, cols = (normed.shape[0], normed.shape[1])
    mixed = jnp.dot(normed.reshape(rows * cols, D), w_qkv, preferred_element_type=jnp.float32)
    mixed = to_windows(mixed.astype(jnp.bfloat16).reshape(rows, cols, 3 * D))
    number = mixed.shape[0]
    parts = mixed.reshape(number, WIN * WIN, 3, HEADS, D // HEADS)
    scores = jnp.einsum(
        "wqhe,wkhe->whqk", parts[:, :, 0], parts[:, :, 1], preferred_element_type=jnp.float32
    ) / math.sqrt(D // HEADS)
    label_win = to_windows(labels[:, :, None])[:, :, 0]
    keep_win = to_windows(keep[:, :, None])[:, :, 0]
    same = label_win[:, :, None] == label_win[:, None, :]
    visible = (keep_win[:, None, :] == 1) | jnp.eye(WIN * WIN, dtype=bool)[None]
    allowed = (same & visible)[:, None]
    scores = jnp.where(allowed, scores, -1e30)
    largest = jnp.max(scores, axis=-1, keepdims=True)
    weights = jnp.exp(scores - largest)
    probs = (weights / jnp.sum(weights, axis=-1, keepdims=True)).astype(jnp.bfloat16)
    attended = jnp.einsum(
        "whqk,wkhe->wqhe", probs, parts[:, :, 2], preferred_element_type=jnp.float32
    ).astype(jnp.bfloat16)
    attended = from_windows(attended.reshape(number, WIN * WIN, D), rows, cols)
    projected = jnp.dot(
        attended.reshape(rows * cols, D), w_proj, preferred_element_type=jnp.float32
    )
    return projected.reshape(rows, cols, D)


def swin_block(grid, labels, keep, w_qkv, w_proj, w_up, w_down, gains):
    rows, cols = (grid.shape[0], grid.shape[1])
    flow = grid.astype(jnp.float32)
    normed = layer_norm(flow, gains[0]).astype(jnp.bfloat16)
    flow = flow + attention(normed, labels, keep, w_qkv, w_proj)
    normed = layer_norm(flow, gains[1]).astype(jnp.bfloat16).reshape(rows * cols, D)
    hidden = jax.nn.gelu(
        jnp.dot(normed, w_up, preferred_element_type=jnp.float32), approximate=True
    )
    hidden = hidden.astype(jnp.bfloat16)
    flow = flow + jnp.dot(hidden, w_down, preferred_element_type=jnp.float32).reshape(rows, cols, D)
    return flow.astype(jnp.bfloat16)


def roll_forward(grid, shift_rows, shift_cols):
    rows, cols, feats = grid.shape
    right = from_behind(grid, "tx", -1)
    wide = jnp.concatenate([grid, right], axis=1)
    below = from_behind(wide, "ty", -1)
    whole = jnp.concatenate([wide, below], axis=0)
    anchor = jnp.zeros((), jnp.int32)
    return lax.dynamic_slice(whole, (shift_rows, shift_cols, anchor), (rows, cols, feats))


def roll_back(grid, shift_rows, shift_cols):
    rows, cols, feats = grid.shape
    left = from_behind(grid, "tx", 1)
    wide = jnp.concatenate([left, grid], axis=1)
    above = from_behind(wide, "ty", 1)
    whole = jnp.concatenate([above, wide], axis=0)
    row_start = rows - shift_rows
    col_start = cols - shift_cols
    anchor = jnp.zeros((), jnp.int32)
    return lax.dynamic_slice(whole, (row_start, col_start, anchor), (rows, cols, feats))


def patches_of(picture):
    rows, cols = picture.shape
    shaped = picture.reshape(rows // PATCH, PATCH, cols // PATCH, PATCH).transpose(0, 2, 1, 3)
    return shaped.reshape(rows // PATCH, cols // PATCH, PATCH * PATCH).astype(jnp.bfloat16)


def image_of(pieces):
    rows, cols = (pieces.shape[0], pieces.shape[1])
    shaped = pieces.reshape(rows, cols, PATCH, PATCH).transpose(0, 2, 1, 3)
    return shaped.reshape(rows * PATCH, cols * PATCH)


def region(index, shift):
    side = N // PATCH
    return jnp.where(index < side - WIN, 0, jnp.where(index < side - shift, 1, 2)).astype(jnp.int32)


def per_device(
    image,
    noise,
    offsets,
    key_mask,
    gains,
    observed,
    vis_weight,
    w_embed,
    w_qkv,
    w_proj,
    w_up,
    w_down,
    w_unembed,
    norm_gains,
):
    rows = image.shape[0] // PATCH
    cols = image.shape[1] // PATCH
    plain = jnp.zeros((rows, cols), jnp.int32)
    all_keep = jnp.ones((rows, cols), jnp.int32)
    row_index = lax.axis_index("ty") * rows + counting(rows)
    col_index = lax.axis_index("tx") * cols + counting(cols)
    state = image
    for step in range(STEPS):
        grad = likelihood(state, gains, observed, vis_weight)
        half = state - STEP_SIZES[step] * grad
        patches = patches_of(half)
        tokens = jnp.dot(
            patches.reshape(rows * cols, PATCH * PATCH), w_embed, preferred_element_type=jnp.float32
        )
        tokens = tokens.astype(jnp.bfloat16).reshape(rows, cols, D)
        first = swin_block(
            tokens, plain, key_mask, w_qkv[0], w_proj[0], w_up[0], w_down[0], norm_gains[0]
        )
        shift_rows = offsets[step, 0]
        shift_cols = offsets[step, 1]
        rolled = roll_forward(first, shift_rows, shift_cols)
        regions = (
            3 * region(row_index, shift_rows)[:, None] + region(col_index, shift_cols)[None, :]
        )
        second = swin_block(
            rolled, regions, all_keep, w_qkv[1], w_proj[1], w_up[1], w_down[1], norm_gains[1]
        )
        restored = roll_back(second, shift_rows, shift_cols)
        estimate = jnp.dot(
            restored.reshape(rows * cols, D), w_unembed, preferred_element_type=jnp.float32
        )
        estimate = image_of(estimate.reshape(rows, cols, PATCH * PATCH))
        state = half - SIGMAS[step] * estimate + SIGMAS[step + 1] * noise[step]
    return state


def solution(mesh):
    in_specs = (
        P("ty", "tx"),
        P(None, "ty", "tx"),
        P(),
        P("ty", "tx"),
        P(None, ("ty", "tx"), None),
        P(None, ("ty", "tx"), None),
        P(("ty", "tx"), None),
        P(),
        P(),
        P(),
        P(),
        P(),
        P(),
        P(),
    )
    out_specs = P("ty", "tx")
    return jax.shard_map(
        per_device, mesh=mesh, in_specs=in_specs, out_specs=out_specs, check_vma=False
    )
```

profile of v0, /device:TPU:0, one launch (start us, length us, event | category | flops | bytes accessed | tf_op | source)
XLA Modules:
  0.0 573.5 jit_solution(18019425069755205345)
XLA Ops:
  1.8 7.0 %all-to-all-start = ((bf16[8,32,512]{2,1,0:T(8,128)(2,1)}), bf16[8,32,512]{2,1,0:T(8,128)(2,1)S(1)}, u32[]{:S(2)}, u32[]{:S(2)}) async-start(bf16[8,32,512]{2,1,0:T(8,128)(2,1)} %bitcast.1), calls=%async_computation | async-start | bytes 524288 | tf_op jit(solution)/shard_map/all_to_all | solution.py:99
  10.5 7.1 %all-to-all-done = bf16[8,32,512]{2,1,0:T(8,128)(2,1)S(1)} async-done(((bf16[8,32,512]{2,1,0:T(8,128)(2,1)}), bf16[8,32,512]{2,1,0:T(8,128)(2,1)S(1)}, u32[]{:S(2)}, u32[]{:S(2)}) %all-to-all-start) | async-done | bytes 262176 | tf_op jit(solution)/shard_map/all_to_all | solution.py:99
  25.5 6.9 %all-to-all-start.1 = ((bf16[128,2,512]{2,1,0:T(2,128)(2,1)}), bf16[128,2,512]{2,1,0:T(2,128)(2,1)S(1)}, u32[]{:S(2)}, u32[]{:S(2)}) async-start(bf16[128,2,512]{2,1,0:T(2,128)(2,1)} %reshape.697), calls=%async_computation.1 | async-start | bytes 524288 | tf_op jit(solution)/shard_map/all_to_all | solution.py:104
  35.7 7.2 %all-to-all-done.1 = bf16[128,2,512]{2,1,0:T(2,128)(2,1)S(1)} async-done(((bf16[128,2,512]{2,1,0:T(2,128)(2,1)}), bf16[128,2,512]{2,1,0:T(2,128)(2,1)S(1)}, u32[]{:S(2)}, u32[]{:S(2)}) %all-to-all-start.1) | async-done | bytes 262176 | tf_op jit(solution)/shard_map/all_to_all | solution.py:104
  42.9 5.1 all-to-all-start.2
  50.9 7.5 %all-to-all-done.2 = bf16[128,2,512]{2,1,0:T(2,128)(2,1)S(1)} async-done(((bf16[128,2,512]{2,1,0:T(2,128)(2,1)}), bf16[128,2,512]{2,1,0:T(2,128)(2,1)S(1)}, u32[]{:S(2)}, u32[]{:S(2)}) %all-to-all-start.2) | async-done | bytes 262176 | tf_op jit(solution)/shard_map/all_to_all | solution.py:107
  69.5 4.7 fusion.263
  96.4 5.7 all-to-all-start.3
  105.4 6.8 %all-to-all-done.3 = bf16[128,2,512]{2,1,0:T(2,128)(2,1)} async-done(((bf16[128,2,512]{2,1,0:T(2,128)(2,1)}), bf16[128,2,512]{2,1,0:T(2,128)(2,1)}, u32[]{:S(2)}, u32[]{:S(2)}) %all-to-all-start.3) | async-done | bytes 262176 | tf_op jit(solution)/shard_map/all_to_all | solution.py:119
  112.2 4.9 all-to-all-start.4
  121.4 6.3 %all-to-all-done.4 = bf16[128,2,512]{2,1,0:T(2,128)(2,1)S(1)} async-done(((bf16[128,2,512]{2,1,0:T(2,128)(2,1)}), bf16[128,2,512]{2,1,0:T(2,128)(2,1)S(1)}, u32[]{:S(2)}, u32[]{:S(2)}) %all-to-all-start.4) | async-done | bytes 262176 | tf_op jit(solution)/shard_map/all_to_all | solution.py:122
  143.9 8.7 %all-to-all-done.5 = bf16[32,8,512]{2,0,1:T(8,128)(2,1)S(1)} async-done(((bf16[32,8,512]{2,0,1:T(8,128)(2,1)}), bf16[32,8,512]{2,0,1:T(8,128)(2,1)S(1)}, u32[]{:S(2)}, u32[]{:S(2)}) %all-to-all-start.5) | async-done | bytes 262176 | tf_op jit(solution)/shard_map/all_to_all | solution.py:127
  165.6 5.0 reshape_reshape.43
  175.5 4.8 fusion.692
  196.7 11.2 %collective-permute-done = bf16[16,32,512]{2,1,0:T(8,128)(2,1)S(1)} collective-permute-done((bf16[16,32,512]{2,1,0:T(8,128)(2,1)S(1)}, bf16[16,32,512]{2,1,0:T(8,128)(2,1)S(1)}, u32[]{:S(2)}, u32[]{:S(2)}) %collective-permute-start) | collective-permute-done | bytes 524320 | tf_op jit(solution)/shard_map/ppermute | solution.py:24
  217.0 4.8 collective-permute-done.1
  252.3 18.6 %collective-permute-done.2 = bf16[16,32,512]{2,1,0:T(8,128)(2,1)S(1)} collective-permute-done((bf16[16,32,512]{2,1,0:T(8,128)(2,1)S(1)}, bf16[16,32,512]{2,1,0:T(8,128)(2,1)S(1)}, u32[]{:S(2)}, u32[]{:S(2)}) %collective-permute-start.2) | collective-permute-done | bytes 524320 | tf_op jit(solution)/shard_map/ppermute | solution.py:24
  276.9 12.1 %collective-permute-done.3 = bf16[16,64,512]{2,1,0:T(8,128)(2,1)S(1)} collective-permute-done((bf16[16,64,512]{2,1,0:T(8,128)(2,1)}, bf16[16,64,512]{2,1,0:T(8,128)(2,1)S(1)}, u32[]{:S(2)}, u32[]{:S(2)}) %collective-permute-start.3) | collective-permute-done | bytes 1048608 | tf_op jit(solution)/shard_map/ppermute | solution.py:24
  301.6 12.0 %all_to_all.100 = bf16[8,32,512]{2,1,0:T(8,128)(2,1)S(1)} all-to-all(bf16[8,32,512]{2,1,0:T(8,128)(2,1)S(1)} %bitcast.846), channel_id=1, replica_groups=mesh['ty'=16,'tx'=8] {'tx'}, dimensions={0} | all-to-all | bytes 524288 | tf_op jit(solution)/shard_map/all_to_all | solution.py:99
  326.4 5.7 all-to-all-start.7
  335.5 6.8 %all-to-all-done.7 = bf16[128,2,512]{2,1,0:T(2,128)(2,1)} async-done(((bf16[128,2,512]{2,1,0:T(2,128)(2,1)}), bf16[128,2,512]{2,1,0:T(2,128)(2,1)}, u32[]{:S(2)}, u32[]{:S(2)}) %all-to-all-start.7) | async-done | bytes 262176 | tf_op jit(solution)/shard_map/all_to_all | solution.py:104
  342.3 4.9 all-to-all-start.8
  352.4 5.3 all-to-all-done.8
  391.4 4.9 all-to-all-start.9
  399.6 7.2 %all-to-all-done.9 = bf16[128,2,512]{2,1,0:T(2,128)(2,1)S(1)} async-done(((bf16[128,2,512]{2,1,0:T(2,128)(2,1)}), bf16[128,2,512]{2,1,0:T(2,128)(2,1)S(1)}, u32[]{:S(2)}, u32[]{:S(2)}) %all-to-all-start.9) | async-done | bytes 262176 | tf_op jit(solution)/shard_map/all_to_all | solution.py:119
  406.8 4.9 all-to-all-start.10
  414.6 7.7 %all-to-all-done.10 = bf16[128,2,512]{2,1,0:T(2,128)(2,1)S(1)} async-done(((bf16[128,2,512]{2,1,0:T(2,128)(2,1)}), bf16[128,2,512]{2,1,0:T(2,128)(2,1)S(1)}, u32[]{:S(2)}, u32[]{:S(2)}) %all-to-all-start.10) | async-done | bytes 262176 | tf_op jit(solution)/shard_map/all_to_all | solution.py:122
  431.6 12.2 %all_to_all.101 = bf16[32,8,512]{2,0,1:T(8,128)(2,1)S(1)} all-to-all(bf16[32,8,512]{2,0,1:T(8,128)(2,1)S(1)} %copy.280), channel_id=1, replica_groups=mesh['ty'=16,'tx'=8] {'tx'}, dimensions={1} | all-to-all | bytes 524288 | tf_op jit(solution)/shard_map/all_to_all | solution.py:127
  478.4 10.7 %collective-permute-done.4 = bf16[16,32,512]{2,1,0:T(8,128)(2,1)S(1)} collective-permute-done((bf16[16,32,512]{2,1,0:T(8,128)(2,1)S(1)}, bf16[16,32,512]{2,1,0:T(8,128)(2,1)S(1)}, u32[]{:S(2)}, u32[]{:S(2)}) %collective-permute-start.4) | collective-permute-done | bytes 524320 | tf_op jit(solution)/shard_map/ppermute | solution.py:24
  493.3 8.5 %collective-permute-done.5 = bf16[16,64,512]{2,1,0:T(8,128)(2,1)S(1)} collective-permute-done((bf16[16,64,512]{2,1,0:T(8,128)(2,1)S(1)}, bf16[16,64,512]{2,1,0:T(8,128)(2,1)S(1)}, u32[]{:S(2)}, u32[]{:S(2)}) %collective-permute-start.5) | collective-permute-done | bytes 1048608 | tf_op jit(solution)/shard_map/ppermute | solution.py:24
  527.8 17.4 %collective-permute-done.6 = bf16[16,32,512]{2,1,0:T(8,128)(2,1)S(1)} collective-permute-done((bf16[16,32,512]{2,1,0:T(8,128)(2,1)S(1)}, bf16[16,32,512]{2,1,0:T(8,128)(2,1)S(1)}, u32[]{:S(2)}, u32[]{:S(2)}) %collective-permute-start.6) | collective-permute-done | bytes 524320 | tf_op jit(solution)/shard_map/ppermute | solution.py:24
  549.3 13.5 %collective-permute-done.7 = bf16[16,64,512]{2,1,0:T(8,128)(2,1)} collective-permute-done((bf16[16,64,512]{2,1,0:T(8,128)(2,1)S(1)}, bf16[16,64,512]{2,1,0:T(8,128)(2,1)}, u32[]{:S(2)}, u32[]{:S(2)}) %collective-permute-start.7) | collective-permute-done | bytes 1048608 | tf_op jit(solution)/shard_map/ppermute | solution.py:24
  (363 shorter events, 300.9 us)
Async XLA Ops:
  0.0 161.1 %copy-start = (bf16[256,512]{1,0:T(8,128)(2,1)S(1)}, bf16[256,512]{1,0:T(8,128)(2,1)}, u32[]{:S(2)}) copy-start(bf16[256,512]{1,0:T(8,128)(2,1)} %param.21) | copy-start | bytes 786436
  1.8 15.7 %all-to-all-start = ((bf16[8,32,512]{2,1,0:T(8,128)(2,1)}), bf16[8,32,512]{2,1,0:T(8,128)(2,1)S(1)}, u32[]{:S(2)}, u32[]{:S(2)}) async-start(bf16[8,32,512]{2,1,0:T(8,128)(2,1)} %bitcast.1), calls=%async_computation | async-start | bytes 524288 | tf_op jit(solution)/shard_map/all_to_all | solution.py:99
  23.9 8.4 %copy-start.27 = (f32[32,128,32]{1,2,0:T(8,128)S(1)}, f32[32,128,32]{1,2,0:T(8,128)}, u32[]{:S(2)}) copy-start(f32[32,128,32]{1,2,0:T(8,128)} %fusion.239) | copy-start | bytes 1572868
  25.5 17.4 %all-to-all-start.1 = ((bf16[128,2,512]{2,1,0:T(2,128)(2,1)}), bf16[128,2,512]{2,1,0:T(2,128)(2,1)S(1)}, u32[]{:S(2)}, u32[]{:S(2)}) async-start(bf16[128,2,512]{2,1,0:T(2,128)(2,1)} %reshape.697), calls=%async_computation.1 | async-start | bytes 524288 | tf_op jit(solution)/shard_map/all_to_all | solution.py:104
  42.9 15.5 %all-to-all-start.2 = ((bf16[128,2,512]{2,1,0:T(2,128)(2,1)}), bf16[128,2,512]{2,1,0:T(2,128)(2,1)S(1)}, u32[]{:S(2)}, u32[]{:S(2)}) async-start(bf16[128,2,512]{2,1,0:T(2,128)(2,1)} %reshape.695), calls=%async_computation.2 | async-start | bytes 524288 | tf_op jit(solution)/shard_map/all_to_all | solution.py:107
  91.5 10.5 %copy-start.3 = (f32[32,32,128]{2,1,0:T(8,128)S(1)}, f32[32,32,128]{2,1,0:T(8,128)}, u32[]{:S(2)}) copy-start(f32[32,32,128]{2,1,0:T(8,128)} %copy-done.2) | copy-start | bytes 1572868
  91.5 10.5 %copy-start.5 = (f32[32,32,128]{2,1,0:T(8,128)S(1)}, f32[32,32,128]{2,1,0:T(8,128)}, u32[]{:S(2)}) copy-start(f32[32,32,128]{2,1,0:T(8,128)} %copy-done.4) | copy-start | bytes 1572868
  93.3 8.7 %copy-start.28 = (f32[32,128,32]{1,2,0:T(8,128)S(1)}, f32[32,128,32]{1,2,0:T(8,128)}, u32[]{:S(2)}) copy-start(f32[32,128,32]{1,2,0:T(8,128)} %fusion.241) | copy-start | bytes 1572868
  96.4 15.8 %all-to-all-start.3 = ((bf16[128,2,512]{2,1,0:T(2,128)(2,1)}), bf16[128,2,512]{2,1,0:T(2,128)(2,1)}, u32[]{:S(2)}, u32[]{:S(2)}) async-start(bf16[128,2,512]{2,1,0:T(2,128)(2,1)} %reshape.701), calls=%async_computation.3 | async-start | bytes 524288 | tf_op jit(solution)/shard_map/all_to_all | solution.py:119
  112.2 15.4 %all-to-all-start.4 = ((bf16[128,2,512]{2,1,0:T(2,128)(2,1)}), bf16[128,2,512]{2,1,0:T(2,128)(2,1)S(1)}, u32[]{:S(2)}, u32[]{:S(2)}) async-start(bf16[128,2,512]{2,1,0:T(2,128)(2,1)} %reshape.699), calls=%async_computation.4 | async-start | bytes 524288 | tf_op jit(solution)/shard_map/all_to_all | solution.py:122
  134.8 18.7 %copy-start.14 = (f32[256,512]{1,0:T(8,128)S(1)}, f32[256,512]{1,0:T(8,128)}, u32[]{:S(2)}) copy-start(f32[256,512]{1,0:T(8,128)} %param.14) | copy-start | bytes 1572868
  139.7 12.9 %all-to-all-start.5 = ((bf16[32,8,512]{2,0,1:T(8,128)(2,1)}), bf16[32,8,512]{2,0,1:T(8,128)(2,1)S(1)}, u32[]{:S(2)}, u32[]{:S(2)}) async-start(bf16[32,8,512]{2,0,1:T(8,128)(2,1)} %copy.234), calls=%async_computation.5 | async-start | bytes 524288 | tf_op jit(solution)/shard_map/all_to_all | solution.py:127
  195.1 14.1 %copy-start.46 = (s32[2,2]{1,0:T(2,128)S(1)}, s32[2,2]{1,0:T(2,128)}, u32[]{:S(2)}) copy-start(s32[2,2]{1,0:T(2,128)} %param.16) | copy-start | bytes 52
  195.1 12.8 %collective-permute-start = (bf16[16,32,512]{2,1,0:T(8,128)(2,1)S(1)}, bf16[16,32,512]{2,1,0:T(8,128)(2,1)S(1)}, u32[]{:S(2)}, u32[]{:S(2)}) collective-permute-start(bf16[16,32,512]{2,1,0:T(8,128)(2,1)S(1)} %fusion.107), channel_id=1, source_target_pairs={{0,7},{1,0},{2,1},{3,2},{4,3},{5,4},{6,5},{7,6},{8,15},{9,8},{10,9... | collective-permute-start | bytes 1572872 | tf_op jit(solution)/shard_map/ppermute | solution.py:24
  209.0 12.8 %collective-permute-start.1 = (bf16[16,64,512]{2,1,0:T(8,128)(2,1)}, bf16[16,64,512]{2,1,0:T(8,128)(2,1)}, u32[]{:S(2)}, u32[]{:S(2)}) collective-permute-start(bf16[16,64,512]{2,1,0:T(8,128)(2,1)} %pad_maximum_fusion), channel_id=1, source_target_pairs={{0,120},{8,0},{16,8},{24,16},{32,24},{40,32},{48,40},{56,48},{64,5... | collective-permute-start | bytes 3145736 | tf_op jit(solution)/shard_map/ppermute | solution.py:24
  217.0 7.0 %copy-start.55 = (bf16[2,512,1536]{2,1,0:T(8,128)(2,1)S(1)}, bf16[2,512,1536]{2,1,0:T(8,128)(2,1)}, u32[]{:S(2)}) copy-start(bf16[2,512,1536]{2,1,0:T(8,128)(2,1)} %param.22) | copy-start | bytes 9437188
  252.2 36.8 %copy-start.31 = (bf16[16,32,512]{2,1,0:T(8,128)(2,1)}, bf16[16,32,512]{2,1,0:T(8,128)(2,1)S(1)}, u32[]{:S(2)}) copy-start(bf16[16,32,512]{2,1,0:T(8,128)(2,1)S(1)} %fusion.101) | copy-start | bytes 1572868
  252.2 18.7 %collective-permute-start.2 = (bf16[16,32,512]{2,1,0:T(8,128)(2,1)S(1)}, bf16[16,32,512]{2,1,0:T(8,128)(2,1)S(1)}, u32[]{:S(2)}, u32[]{:S(2)}) collective-permute-start(bf16[16,32,512]{2,1,0:T(8,128)(2,1)S(1)} %fusion.101), channel_id=1, source_target_pairs={{0,1},{1,2},{2,3},{3,4},{4,5},{5,6},{6,7},{7,0},{8,9},{9,10},{10,1... | collective-permute-start | bytes 1572872 | tf_op jit(solution)/shard_map/ppermute | solution.py:24
  270.9 18.1 %copy-start.33 = (bf16[16,32,512]{2,1,0:T(8,128)(2,1)}, bf16[16,32,512]{2,1,0:T(8,128)(2,1)S(1)}, u32[]{:S(2)}) copy-start(bf16[16,32,512]{2,1,0:T(8,128)(2,1)S(1)} %collective-permute-done.2) | copy-start | bytes 1572868
  272.1 16.9 %collective-permute-start.3 = (bf16[16,64,512]{2,1,0:T(8,128)(2,1)}, bf16[16,64,512]{2,1,0:T(8,128)(2,1)S(1)}, u32[]{:S(2)}, u32[]{:S(2)}) collective-permute-start(bf16[16,64,512]{2,1,0:T(8,128)(2,1)} %pad_maximum_fusion.1), channel_id=1, source_target_pairs={{0,8},{8,16},{16,24},{24,32},{32,40},{40,48},{48,56},{56,64},{64,7... | collective-permute-start | bytes 3145736 | tf_op jit(solution)/shard_map/ppermute | solution.py:24
  323.4 8.7 %copy-start.29 = (f32[32,128,32]{1,2,0:T(8,128)S(1)}, f32[32,128,32]{1,2,0:T(8,128)}, u32[]{:S(2)}) copy-start(f32[32,128,32]{1,2,0:T(8,128)} %fusion.243) | copy-start | bytes 1572868
  326.4 15.8 %all-to-all-start.7 = ((bf16[128,2,512]{2,1,0:T(2,128)(2,1)}), bf16[128,2,512]{2,1,0:T(2,128)(2,1)}, u32[]{:S(2)}, u32[]{:S(2)}) async-start(bf16[128,2,512]{2,1,0:T(2,128)(2,1)} %reshape.705), calls=%async_computation.7 | async-start | bytes 524288 | tf_op jit(solution)/shard_map/all_to_all | solution.py:104
  342.3 15.4 %all-to-all-start.8 = ((bf16[128,2,512]{2,1,0:T(2,128)(2,1)}), bf16[128,2,512]{2,1,0:T(2,128)(2,1)S(1)}, u32[]{:S(2)}, u32[]{:S(2)}) async-start(bf16[128,2,512]{2,1,0:T(2,128)(2,1)} %reshape.703), calls=%async_computation.8 | async-start | bytes 524288 | tf_op jit(solution)/shard_map/all_to_all | solution.py:107
  391.4 15.4 %all-to-all-start.9 = ((bf16[128,2,512]{2,1,0:T(2,128)(2,1)}), bf16[128,2,512]{2,1,0:T(2,128)(2,1)S(1)}, u32[]{:S(2)}, u32[]{:S(2)}) async-start(bf16[128,2,512]{2,1,0:T(2,128)(2,1)} %reshape.709), calls=%async_computation.9 | async-start | bytes 524288 | tf_op jit(solution)/shard_map/all_to_all | solution.py:119
  406.8 15.5 %all-to-all-start.10 = ((bf16[128,2,512]{2,1,0:T(2,128)(2,1)}), bf16[128,2,512]{2,1,0:T(2,128)(2,1)S(1)}, u32[]{:S(2)}, u32[]{:S(2)}) async-start(bf16[128,2,512]{2,1,0:T(2,128)(2,1)} %reshape.707), calls=%async_computation.10 | async-start | bytes 524288 | tf_op jit(solution)/shard_map/all_to_all | solution.py:122
  427.4 17.3 %copy-start.12 = (f32[256,512]{1,0:T(8,128)S(1)}, f32[256,512]{1,0:T(8,128)}, u32[]{:S(2)}) copy-start(f32[256,512]{1,0:T(8,128)} %get-tuple-element.11) | copy-start | bytes 1572868
  476.8 12.3 %collective-permute-start.4 = (bf16[16,32,512]{2,1,0:T(8,128)(2,1)S(1)}, bf16[16,32,512]{2,1,0:T(8,128)(2,1)S(1)}, u32[]{:S(2)}, u32[]{:S(2)}) collective-permute-start(bf16[16,32,512]{2,1,0:T(8,128)(2,1)S(1)} %fusion.104), channel_id=1, source_target_pairs={{0,7},{1,0},{2,1},{3,2},{4,3},{5,4},{6,5},{7,6},{8,15},{9,8},{10,9... | collective-permute-start | bytes 1572872 | tf_op jit(solution)/shard_map/ppermute | solution.py:24
  489.2 12.6 %collective-permute-start.5 = (bf16[16,64,512]{2,1,0:T(8,128)(2,1)S(1)}, bf16[16,64,512]{2,1,0:T(8,128)(2,1)S(1)}, u32[]{:S(2)}, u32[]{:S(2)}) collective-permute-start(bf16[16,64,512]{2,1,0:T(8,128)(2,1)S(1)} %pad_maximum_fusion.2), channel_id=1, source_target_pairs={{0,120},{8,0},{16,8},{24,16},{32,24},{40,32},{48,40},{56,48},{64,5... | collective-permute-start | bytes 3145736 | tf_op jit(solution)/shard_map/ppermute | solution.py:24
  493.3 10.3 %copy-start.56 = (bf16[2,512,1536]{2,1,0:T(8,128)(2,1)S(1)}, bf16[2,512,1536]{2,1,0:T(8,128)(2,1)}, u32[]{:S(2)}) copy-start(bf16[2,512,1536]{2,1,0:T(8,128)(2,1)} %param.22) | copy-start | bytes 9437188
  527.5 35.3 %copy-start.24 = (bf16[512,256]{0,1:T(8,128)(2,1)S(1)}, bf16[512,256]{0,1:T(8,128)(2,1)}, u32[]{:S(2)}) copy-start(bf16[512,256]{0,1:T(8,128)(2,1)} %copy.251) | copy-start | bytes 786436
  527.5 17.7 %collective-permute-start.6 = (bf16[16,32,512]{2,1,0:T(8,128)(2,1)S(1)}, bf16[16,32,512]{2,1,0:T(8,128)(2,1)S(1)}, u32[]{:S(2)}, u32[]{:S(2)}) collective-permute-start(bf16[16,32,512]{2,1,0:T(8,128)(2,1)S(1)} %fusion.98), channel_id=1, source_target_pairs={{0,1},{1,2},{2,3},{3,4},{4,5},{5,6},{6,7},{7,0},{8,9},{9,10},{10,1... | collective-permute-start | bytes 1572872 | tf_op jit(solution)/shard_map/ppermute | solution.py:24
  546.1 16.7 %collective-permute-start.7 = (bf16[16,64,512]{2,1,0:T(8,128)(2,1)S(1)}, bf16[16,64,512]{2,1,0:T(8,128)(2,1)}, u32[]{:S(2)}, u32[]{:S(2)}) collective-permute-start(bf16[16,64,512]{2,1,0:T(8,128)(2,1)S(1)} %pad_maximum_fusion.3), channel_id=1, source_target_pairs={{0,8},{8,16},{16,24},{24,32},{32,40},{40,48},{48,56},{56,64},{64,7... | collective-permute-start | bytes 3145736 | tf_op jit(solution)/shard_map/ppermute | solution.py:24
  (43 other events, 126.2 us)
where the time goes:
time: 583 us; the launch traced here: 573 us
  waiting for transfers between devices  167 us (29%)
  local copies, waits for them, and re-layouts  151 us (26%)
  matrix products  131 us (22%)
  starting transfers between devices  59.2 us (10%)
  other arithmetic  24.3 us (4%)
  blocking collectives  24.2 us (4%)
  between operations  16.6 us (3%)
    ppermute x8, waiting for transfers between devices, from_behind(): lax.ppermute(shard, axis, [(i, (i + by) % size) for i in range(size)])  96.9 us
    unnamed x135, local copies, waits for them, and re-layouts  40.8 us
    another operation x4, local copies, waits for them, and re-layouts, attention(): parts = mixed.reshape(number, WIN * WIN, 3, HEADS, D // HEADS)  16.1 us
    dot_general x8, matrix products, complex_einsum(): jnp.einsum(form, left[0], right[1], precision=HIGHEST)  15.8 us
    mul x4, local copies, waits for them, and re-layouts, per_device(): state = half - SIGMAS[step] * estimate + SIGMAS[step + 1] * noise[step]  14.8 us
    sub x4, matrix products, attention(): weights = jnp.exp(scores - largest)  14.1 us
    all_to_all x2, waiting for transfers between devices, likelihood(): lax.all_to_all(spec_re.astype(jnp.bfloat16), ('ty', 'tx'), split_axis=1,...  14 us
    all_to_all x2, waiting for transfers between devices, likelihood(): lax.all_to_all(wave_re.astype(jnp.bfloat16), ('ty', 'tx'), split_axis=1,...  14 us
  transfers between devices with their start and end apart: 18, of which 18 were waited for; matrix products, arithmetic and copies ran while one was open for 6% of the time, Pallas kernels for 0%

commit v1 on v0

v1 whole, which is shorter than its diff:
```python
import functools
import math

import jax
import jax.numpy as jnp
import numpy as np
from jax import lax
from jax.experimental import pallas as pl
from jax.experimental.pallas import tpu as pltpu
from jax.sharding import PartitionSpec as P

N = 4096
WIN = 8
D = 512
HEADS = 8
FF = 2048
STEPS = 2
NTY = 16
NTX = 8
DEV = NTY * NTX
ROWS = 16
COLS = 32
TOKENS = ROWS * COLS
PIX = 256
SIDE = 256
SIGMAS = (0.8, 0.5, 0.3)
STEP_SIZES = (0.9, 0.7)
EPSILON = 1e-05
MESH = pl.DeviceIdType.MESH
F32 = jnp.float32
BF16 = jnp.bfloat16


def tables():
    k1 = np.array([32 * t + 16 * h + m for h in range(2) for t in range(8) for m in range(16)])
    k = np.arange(256)
    ang = 2 * np.pi * ((k1[:, None] * k[None, :]) % 256) / 256
    w1 = np.concatenate([np.cos(ang), -np.sin(ang)], axis=0)
    w4 = w1.T
    b = np.tile(np.arange(16), 16)
    ang = 2 * np.pi * (k1[:, None] * b[None, :]) / 4096
    tw1 = np.stack([np.cos(ang), np.sin(ang)])
    eye = np.eye(32)
    b16 = np.arange(16)
    ang = 2 * np.pi * ((b16[:, None] * b16[None, :]) % 16) / 16
    wr, wi = np.cos(ang), -np.sin(ang)
    core = np.zeros((2, 16, 16, 2))
    core[0, :, :, 0], core[0, :, :, 1] = wr, wi
    core[1, :, :, 0], core[1, :, :, 1] = -wi, wr
    core = core.reshape(2, 16, 8, 2, 2)
    f1 = np.einsum("cbpld,xy->cxbpdly", core, eye).reshape(1024, 1024)
    wi = -wi
    core = np.zeros((16, 2, 2, 16))
    core[:, 0, 0], core[:, 0, 1] = wr, wi
    core[:, 1, 0], core[:, 1, 1] = -wi, wr
    core = core.reshape(8, 2, 2, 2, 16)
    f2 = np.einsum("plcdb,xy->pclxdyb", core, eye).reshape(1024, 1024)
    u = np.arange(128)
    ang = 2 * np.pi * ((u[:, None] * u[None, :]) % 128) / 128
    w2 = np.concatenate([np.cos(ang), -np.sin(ang)], axis=1)
    w3 = np.concatenate([np.cos(ang), np.sin(ang)], axis=1)
    rho = np.arange(32)
    ang = 2 * np.pi * (rho[:, None] * u[None, :]) / 4096
    c, s = np.cos(ang), np.sin(ang)
    tw2c = np.concatenate([c, c, c, c], axis=0).T
    tw2s = np.concatenate([s, s, -s, -s], axis=0).T
    tw2 = np.stack([tw2c, tw2s])
    tw3 = np.stack([np.concatenate([c, c]), np.concatenate([s, s])]) / N
    ang = 2 * np.pi * ((rho[:, None] * rho[None, :]) % 32) / 32
    wr, wi = np.cos(ang), -np.sin(ang)
    eye2 = np.eye(2)

    def block(wr, wi):
        return np.block([[np.kron(eye2, wr), np.kron(eye2, -wi)], [np.kron(eye2, wi), np.kron(eye2, wr)]])

    m2 = block(wr, wi)
    m3 = block(wr, -wi)
    half = lambda x: np.asarray(x, np.float32).astype(BF16)
    full = lambda x: np.asarray(x, np.float32)
    return (half(w1), half(w4), full(tw1), half(f1), half(f2), half(w2), half(w3), full(tw2), full(tw3), half(m2), half(m3))


def mm(a, b):
    return jnp.dot(a, b, preferred_element_type=F32)


def nt(a, b):
    return lax.dot_general(a, b, (((1,), (1,)), ((), ())), preferred_element_type=F32)


def swap_blocks(x):
    sub = lax.broadcasted_iota(jnp.int32, x.shape, 1)
    lane = lax.broadcasted_iota(jnp.int32, x.shape, 2) // 16
    for d in (4, 2, 1):
        bs = (sub // d) % 2
        bl = (lane // d) % 2
        after = pltpu.roll(pltpu.roll(x, 8 - d, 1), 16 * d, 2)
        if d == 4:
            x = jnp.where(bs == bl, x, after)
        else:
            before = pltpu.roll(pltpu.roll(x, d, 1), 128 - 16 * d, 2)
            x = jnp.where(bs == bl, x, jnp.where(bs == 0, after, before))
    return x


def pixels_to_patches(read, write):
    for i in range(ROWS):
        pieces = [read(i * 16 + ah * 8, kh * 128) for kh in range(4) for ah in range(2)]
        out = swap_blocks(jnp.stack(pieces))
        for kh in range(4):
            for ah in range(2):
                write(i * COLS + kh * 8, ah * 128, out[kh * 2 + ah])


def patches_to_pixels(read, write):
    for i in range(ROWS):
        pieces = [read(i * COLS + kh * 8, ah * 128) for kh in range(4) for ah in range(2)]
        out = swap_blocks(jnp.stack(pieces))
        for kh in range(4):
            for ah in range(2):
                write(i * 16 + ah * 8, kh * 128, out[kh * 2 + ah])


def coords(d):
    return (d // NTX, lax.rem(d, NTX))


def exchange(mine, count, peer, src, dst, send_sem, recv_sem):
    def send(o, carry):
        t = lax.rem(mine + o, count)
        pltpu.make_async_remote_copy(
            src.at[t], dst.at[mine], send_sem, recv_sem, device_id=peer(t), device_id_type=MESH
        ).start()
        return carry

    lax.fori_loop(1, count, send, 0)
    dst[mine] = src[mine]
    rest = pltpu.make_async_remote_copy(
        src.at[pl.ds(0, count - 1)],
        dst.at[pl.ds(0, count - 1)],
        send_sem,
        recv_sem,
        device_id=peer(lax.rem(mine + 1, count)),
        device_id_type=MESH,
    )
    rest.wait_send()
    rest.wait_recv()


def layer_norm(values, gain):
    centre = jnp.mean(values, axis=-1, keepdims=True)
    shifted = values - centre
    spread = jnp.mean(shifted * shifted, axis=-1, keepdims=True)
    return shifted * lax.rsqrt(spread + EPSILON) * gain


def gelu(v):
    return 0.5 * v * (1.0 + jnp.tanh(math.sqrt(2.0 / math.pi) * (v + 0.044715 * (v * v * v))))


def swin_block(flow, qkv, att, allowed_of, w_qkv, w_proj, w_up, w_down, gains, j):
    gain0 = gains[j, 0:1, :]
    gain1 = gains[j, 1:2, :]
    normed = layer_norm(flow[...], gain0).astype(BF16)
    qkv[...] = mm(normed, w_qkv[j]).astype(BF16)
    lane_head = lax.broadcasted_iota(jnp.int32, (HEADS, 1, D), 2) // 64
    head = lax.broadcasted_iota(jnp.int32, (HEADS, 1, D), 0)
    own = lane_head == head
    own16 = jnp.where(own, 1.0, 0.0).astype(BF16)

    def window(w, carry):
        rows = pl.ds(pl.multiple_of(w * 64, 64), 64)
        q = qkv[rows, 0:D]
        k = qkv[rows, D : 2 * D]
        v = qkv[rows, 2 * D : 3 * D]
        spread_q = (q[None] * own16).reshape(HEADS * 64, D)
        scores = nt(spread_q, k).reshape(HEADS, 64, 64) * 0.125
        scores = jnp.where(allowed_of(w)[None], scores, -1e30)
        largest = jnp.max(scores, axis=-1, keepdims=True)
        weights = jnp.exp(scores - largest)
        probs = (weights / jnp.sum(weights, axis=-1, keepdims=True)).astype(BF16)
        mixed = mm(probs.reshape(HEADS * 64, 64), v).reshape(HEADS, 64, D)
        att[rows, :] = jnp.sum(jnp.where(own, mixed, 0.0), axis=0).astype(BF16)
        return carry

    lax.fori_loop(0, 8, window, 0)
    after = flow[...] + mm(att[...], w_proj[j])
    normed = layer_norm(after, gain1).astype(BF16)
    for c in range(0, FF, 512):
        hidden = gelu(mm(normed, w_up[j, :, c : c + 512])).astype(BF16)
        after = after + mm(hidden, w_down[j, c : c + 512, :])
    flow[...] = after


def region(index, shift):
    return jnp.where(index < SIDE - WIN, 0, jnp.where(index < SIDE - shift, 1, 2))


def windows():
    return [(wi, wk, p, ((wi * 4 + wk) * 8 + p) * 8) for wi in range(2) for wk in range(4) for p in range(8)]


def kernel(
    offsets, image, noise, keep, norm_gains,
    w1, w4, tw1, w2, w3, tw2, tw3, m2, m3,
    gains_h, observed_h, weight_h, f1_h, f2_h, w_embed_h, w_qkv_h, w_proj_h, w_up_h, w_down_h, w_unembed_h,
    out,
    gains, observed, weight, f1, f2, w_embed, w_qkv, w_proj, w_up, w_down, w_unembed,
    state, half, sa, ra, sb, rb, sc, rc, sd, rd, xf, xg, big, abr, flow, qkv, att, first, padded, around,
    from_right, from_below, from_corner, to_right, to_below, to_corner, est,
    load_sem, send_sem, recv_sem,
):
    ty = lax.axis_index("ty")
    tx = lax.axis_index("tx")
    me = ty * NTX + tx
    barrier = pltpu.get_barrier_semaphore()

    def greet(o, carry):
        pl.semaphore_signal(barrier, inc=1, device_id=coords(lax.rem(me + o, DEV)), device_id_type=MESH)
        return carry

    lax.fori_loop(1, DEV, greet, 0)
    pairs = [
        (f1_h, f1), (gains_h, gains), (observed_h, observed), (weight_h, weight), (f2_h, f2), (w_embed_h, w_embed),
        (w_qkv_h, w_qkv), (w_proj_h, w_proj), (w_up_h, w_up), (w_down_h, w_down), (w_unembed_h, w_unembed),
    ]
    loads = [pltpu.make_async_copy(a, b, load_sem.at[n]) for n, (a, b) in enumerate(pairs)]
    for load in loads:
        load.start()

    def put_state(row, lane, piece):
        state[row : row + 8, lane : lane + 128] = piece

    pixels_to_patches(lambda r, c: image[r : r + 8, c : c + 128], put_state)
    lane = lax.broadcasted_iota(jnp.int32, (128, 128), 1)
    low = (lane // 32) % 2 == 0
    sign = jnp.where(lane < 64, -1.0, 1.0)
    right = lax.rem(tx + 1, NTX)
    left = lax.rem(tx + NTX - 1, NTX)
    below = lax.rem(ty + 1, NTY)
    above = lax.rem(ty + NTY - 1, NTY)

    for t in range(STEPS):
        base = t * 10

        sa[...] = state[...].astype(BF16).reshape(NTX, 64, PIX)
        if t == 0:
            pl.semaphore_wait(barrier, DEV - 1)
        exchange(tx, NTX, lambda n: (ty, n), sa, ra.at[t], send_sem.at[base], recv_sem.at[base])
        got = ra[t]
        slab = jnp.concatenate([got[:, :32, :].reshape(256, PIX), got[:, 32:, :].reshape(256, PIX)], axis=1)
        cos1 = jnp.concatenate([tw1[0], tw1[0]], axis=1)
        sin1 = jnp.concatenate([tw1[1], tw1[1]], axis=1)
        part = mm(w1[...], slab)
        pr, pi = part[:256], part[256:]
        part = jnp.concatenate([pr * cos1 + pi * sin1, pi * cos1 - pr * sin1], axis=1).astype(BF16)
        if t == 0:
            loads[0].wait()
        big[...] = mm(part, f1[...])
        for p in range(8):
            a0 = big[0:128, p * 128 : p * 128 + 128]
            a1 = big[128:256, p * 128 : p * 128 + 128]
            sb[p * 16 : p * 16 + 8] = jnp.where(low, a0, pltpu.roll(a1, 32, 1)).astype(BF16).reshape(8, 16, 128)
            sb[p * 16 + 8 : p * 16 + 16] = jnp.where(low, pltpu.roll(a0, 96, 1), a1).astype(BF16).reshape(8, 16, 128)
        exchange(me, DEV, coords, sb, rb.at[t], send_sem.at[base + 1], recv_sem.at[base + 1])

        if t == 0:
            for n in (1, 2, 3):
                loads[n].wait()
            for q in range(4):
                rows = slice(q * 8, q * 8 + 8)
                for v in range(32):
                    cols = slice(v * 128, v * 128 + 128)
                    gr, gi = gains[0, rows, cols], gains[1, rows, cols]
                    zr, zi = observed[0, rows, cols], observed[1, rows, cols]
                    wt = weight[rows, cols]
                    at = slice((q * 32 + v) * 8, (q * 32 + v) * 8 + 8)
                    xf[at, :] = (wt * (gr * gr + gi * gi)) * (1.0 / N)
                    xf[1024 + at.start : 1024 + at.stop, :] = wt * (gr * zr + gi * zi)
                    xg[at, :] = wt * (gr * zi - gi * zr)
            for q in range(4):
                h, mh = q // 2, q % 2
                for ml in range(8):
                    cols = slice((mh * 8 + ml) * 128, (mh * 8 + ml) * 128 + 128)
                    abr[0, h * 32 : h * 32 + 32, cols] = xf[pl.ds(q * 256 + ml, 32, stride=8), :]
                    abr[1, h * 32 : h * 32 + 32, cols] = xf[pl.ds(1024 + q * 256 + ml, 32, stride=8), :]
                    abr[2, h * 32 : h * 32 + 32, cols] = xg[pl.ds(q * 256 + ml, 32, stride=8), :]

        xf[...] = rb[t].reshape(DEV * 16, 128).astype(F32)
        for m4 in range(0, 16, 4):
            xs = [xf[pl.ds(m4 + n, DEV, stride=16), :] for n in range(4)]
            turned = [pltpu.roll(x, 64, 1) * sign for x in xs]
            both = jnp.concatenate([jnp.concatenate(xs, axis=1), jnp.concatenate(turned, axis=1)], axis=0).astype(BF16)
            y = mm(w2[...], both)
            ys = [y[:, n * 128 : n * 128 + 128] for n in range(4)]
            ys = [x * tw2[0] + pltpu.roll(x, 64, 1) * tw2[1] for x in ys]
            z = nt(m2[...], jnp.concatenate(ys, axis=0).astype(BF16))
            cols = slice(m4 * 128, m4 * 128 + 512)
            fac = abr[0, :, cols]
            back = jnp.concatenate([fac * z[:64] - abr[1, :, cols], fac * z[64:] - abr[2, :, cols]], axis=0)
            v = mm(m3[...], back.astype(BF16))
            rows = []
            for n in range(4):
                vr, vi = v[:64, n * 128 : n * 128 + 128], v[64:, n * 128 : n * 128 + 128]
                xr = vr * tw3[0] - vi * tw3[1]
                xi = vi * tw3[0] + vr * tw3[1]
                rows.append(jnp.concatenate([jnp.concatenate([xr, xi], axis=0), jnp.concatenate([-xi, xr], axis=0)], axis=1))
            u = nt(w3[...], jnp.concatenate(rows, axis=0).astype(BF16))
            for n in range(4):
                xf[pl.ds(m4 + n, DEV, stride=16), :] = u[:, n * 128 : n * 128 + 128]
        sc[...] = xf[...].astype(BF16).reshape(DEV, 16, 128)
        exchange(me, DEV, coords, sc, rc.at[t], send_sem.at[base + 2], recv_sem.at[base + 2])

        for p in range(8):
            r0 = rc[t, p * 16 : p * 16 + 8].reshape(128, 128).astype(F32)
            r1 = rc[t, p * 16 + 8 : p * 16 + 16].reshape(128, 128).astype(F32)
            big[0:128, p * 128 : p * 128 + 128] = jnp.where(low, r0, pltpu.roll(r1, 32, 1))
            big[128:256, p * 128 : p * 128 + 128] = jnp.where(low, pltpu.roll(r0, 96, 1), r1)
        if t == 0:
            loads[4].wait()
        part = mm(big[...].astype(BF16), f2[...])
        pr, pi = part[:, :512], part[:, 512:]
        part = jnp.concatenate([pr * cos1 - pi * sin1, pi * cos1 + pr * sin1], axis=0)
        y = mm(w4[...], part.astype(BF16)).astype(BF16)
        for n in range(NTX):
            sd[n, 0:32, :] = y[n * 32 : n * 32 + 32, :PIX]
            sd[n, 32:64, :] = y[n * 32 : n * 32 + 32, PIX:]
        exchange(tx, NTX, lambda n: (ty, n), sd, rd.at[t], send_sem.at[base + 3], recv_sem.at[base + 3])
        half[...] = state[...] - STEP_SIZES[t] * rd[t].reshape(TOKENS, PIX).astype(F32)

        if t == 0:
            for n in (5, 6, 7, 8, 9, 10):
                loads[n].wait()
        for wi, wk, p, row in windows():
            at = (wi * 8 + p) * COLS + wk * 8
            est[row : row + 8, :] = half[at : at + 8, :]
        flow[...] = mm(est[...].astype(BF16), w_embed[...]).astype(BF16).astype(F32)

        def kept(w):
            row = lax.broadcasted_iota(jnp.int32, (64, 64), 0)
            col = lax.broadcasted_iota(jnp.int32, (64, 64), 1)
            return (keep[pl.ds(w, 1), :] == 1) | (row == col)

        swin_block(flow, qkv, att, kept, w_qkv, w_proj, w_up, w_down, norm_gains, 0)
        first[...] = flow[...].astype(BF16)
        sr = offsets[t, 0]
        sc_ = offsets[t, 1]
        sends = []

        def send(src, dst, who, n):
            copy = pltpu.make_async_remote_copy(
                src, dst, send_sem.at[base + n], recv_sem.at[base + n], device_id=who, device_id_type=MESH
            )
            copy.start()
            sends.append(copy)

        send(first.at[pl.ds(0, 256)], from_below.at[t], (above, tx), 4)
        att[0:64, :] = first[0:64, :]
        att[64:128, :] = first[256:320, :]
        send(att.at[pl.ds(0, 128)], from_right.at[t], (ty, left), 5)
        send(first.at[pl.ds(0, 64)], from_corner.at[t], (above, left), 6)
        for wi, wk, p, row in windows():
            padded[wi * 8 + p, wk * 8 : wk * 8 + 8, :] = first[row : row + 8, :].astype(F32)
        for copy in sends:
            copy.wait()
        for wi, wk, p, row in windows():
            if wi == 0:
                padded[16 + p, wk * 8 : wk * 8 + 8, :] = from_below[t, row : row + 8, :].astype(F32)
            if wk == 0:
                at = (wi * 8 + p) * 8
                padded[wi * 8 + p, 32:40, :] = from_right[t, at : at + 8, :].astype(F32)
            if wi == 0 and wk == 0:
                padded[16 + p, 32:40, :] = from_corner[t, row : row + 8, :].astype(F32)
        for i in range(ROWS):
            rolled = pltpu.roll(padded[i + sr], COLS + 8 - sc_, 0)
            for wk in range(4):
                row = ((i // 8 * 4 + wk) * 8 + i % 8) * 8
                flow[row : row + 8, :] = rolled[wk * 8 : wk * 8 + 8, :]

        def same(w):
            wi = w // 4
            wk = lax.rem(w, 4)
            row = lax.broadcasted_iota(jnp.int32, (64, 64), 0)
            col = lax.broadcasted_iota(jnp.int32, (64, 64), 1)

            def label(x):
                i = ty * ROWS + wi * 8 + x // 8
                k = tx * COLS + wk * 8 + x % 8
                return 3 * region(i, sr) + region(k, sc_)

            return label(row) == label(col)

        swin_block(flow, qkv, att, same, w_qkv, w_proj, w_up, w_down, norm_gains, 1)
        est[...] = mm(flow[...].astype(BF16), w_unembed[...])
        sends.clear()
        sa.reshape(TOKENS, PIX)[...] = est[...].astype(BF16)
        for wi, wk, p, row in windows():
            around[8 + wi * 8 + p, 8 + wk * 8 : 16 + wk * 8, :] = est[row : row + 8, :]
        sd[0] = sa[3]
        sd[1] = sa[7]
        send(sd.at[pl.ds(0, 2)], to_right.at[t], (ty, right), 7)
        send(sa.at[pl.ds(4, 4)], to_below.at[t], (below, tx), 8)
        send(sa.at[7], to_corner.at[t], (below, right), 9)
        for copy in sends:
            copy.wait()
        for p in range(8):
            for wi in range(2):
                around[8 + wi * 8 + p, 0:8, :] = to_right[t, wi, p * 8 : p * 8 + 8, :].astype(F32)
            for wk in range(4):
                around[p, 8 + wk * 8 : 16 + wk * 8, :] = to_below[t, wk, p * 8 : p * 8 + 8, :].astype(F32)
            around[p, 0:8, :] = to_corner[t, p * 8 : p * 8 + 8, :].astype(F32)
        for i in range(ROWS):
            rows = slice(i * COLS, i * COLS + COLS)
            piece = pltpu.roll(around[8 + i - sr], COLS + sc_, 0)[:COLS]
            state[rows, :] = half[rows, :] - SIGMAS[t] * piece
        if t + 1 < STEPS:

            def add_noise(row, lane, piece):
                state[row : row + 8, lane : lane + 128] = state[row : row + 8, lane : lane + 128] + SIGMAS[t + 1] * piece

            pixels_to_patches(lambda r, c: noise[t, r : r + 8, c : c + 128], add_noise)
        else:

            def give(row, lane, piece):
                out[row : row + 8, lane : lane + 128] = piece + SIGMAS[t + 1] * noise[t, row : row + 8, lane : lane + 128]

            patches_to_pixels(lambda r, c: state[r : r + 8, c : c + 128], give)


def per_device(consts, image, noise, offsets, key_mask, gains, observed, vis_weight, w_embed, w_qkv, w_proj, w_up, w_down, w_unembed, norm_gains):
    w1, w4, tw1, f1, f2, w2, w3, tw2, tw3, m2, m3 = consts
    keep = key_mask.reshape(2, 8, 4, 8).transpose(0, 2, 1, 3).reshape(8, 64)
    vmem = pl.BlockSpec(memory_space=pltpu.VMEM)
    hbm = pl.BlockSpec(memory_space=pl.ANY)
    smem = pl.BlockSpec(memory_space=pltpu.SMEM)
    moved = (gains, observed, vis_weight, f1, f2, w_embed, w_qkv, w_proj, w_up, w_down, w_unembed)
    held = [pltpu.VMEM(x.shape, x.dtype) for x in moved]
    V = pltpu.VMEM
    scratch = held + [
        V((TOKENS, PIX), F32),
        V((TOKENS, PIX), F32),
        V((NTX, 64, PIX), BF16),
        V((STEPS, NTX, 64, PIX), BF16),
        V((DEV, 16, 128), BF16),
        V((STEPS, DEV, 16, 128), BF16),
        V((DEV, 16, 128), BF16),
        V((STEPS, DEV, 16, 128), BF16),
        V((NTX, 64, PIX), BF16),
        V((STEPS, NTX, 64, PIX), BF16),
        V((DEV * 16, 128), F32),
        V((1024, 128), F32),
        V((256, 1024), F32),
        V((3, 64, 2048), F32),
        V((TOKENS, D), F32),
        V((TOKENS, 3 * D), BF16),
        V((TOKENS, D), BF16),
        V((TOKENS, D), BF16),
        V((ROWS + 8, COLS + 8, D), F32),
        V((ROWS + 8, COLS + 8, PIX), F32),
        V((STEPS, 128, D), BF16),
        V((STEPS, 256, D), BF16),
        V((STEPS, 64, D), BF16),
        V((STEPS, 2, 64, PIX), BF16),
        V((STEPS, 4, 64, PIX), BF16),
        V((STEPS, 64, PIX), BF16),
        V((TOKENS, PIX), F32),
        pltpu.SemaphoreType.DMA((len(moved),)),
        pltpu.SemaphoreType.DMA((STEPS * 10,)),
        pltpu.SemaphoreType.DMA((STEPS * 10,)),
    ]
    return pl.pallas_call(
        kernel,
        out_shape=jax.ShapeDtypeStruct(image.shape, F32),
        in_specs=[smem] + [vmem] * 13 + [hbm] * len(moved),
        out_specs=vmem,
        scratch_shapes=scratch,
        compiler_params=pltpu.CompilerParams(collective_id=0, has_side_effects=True, vmem_limit_bytes=60 * 2**20),
    )(
        offsets, image, noise, keep, norm_gains,
        w1, w4, tw1, w2, w3, tw2, tw3, m2, m3,
        *moved,
    )


def solution(mesh):
    consts = tables()
    in_specs = (
        P("ty", "tx"),
        P(None, "ty", "tx"),
        P(),
        P("ty", "tx"),
        P(None, ("ty", "tx"), None),
        P(None, ("ty", "tx"), None),
        P(("ty", "tx"), None),
        P(),
        P(),
        P(),
        P(),
        P(),
        P(),
        P(),
    )
    consts_specs = (P(),) * len(consts)
    mapped = jax.shard_map(
        lambda c, *args: per_device(c, *args),
        mesh=mesh,
        in_specs=(consts_specs,) + in_specs,
        out_specs=P("ty", "tx"),
        check_vma=False,
    )
    return lambda *args: mapped(tuple(jnp.asarray(c) for c in consts), *args)
```

time: 583 us -> 174 us (0.30); the launches traced: 573 us -> 173 us
  Pallas kernels: 0 us -> 169 us
  waiting for transfers between devices: 167 us -> 0 us
  local copies, waits for them, and re-layouts: 151 us -> 3.32 us
  matrix products: 131 us -> 0 us
  starting transfers between devices: 59.2 us -> 0 us
  other arithmetic: 24.3 us -> 0 us
  blocking collectives: 24.2 us -> 0 us
  between operations: 16.6 us -> 0.02 us
    pallas_call x0 -> x1, Pallas kernels: none -> 169 us  [per_device(): pl.pallas_call(kernel, out_shape=jax.ShapeDtypeStruct(image.shape, F32),...]
    dot_general x62 -> x0, matrix products: 105 us -> none  [the longest x8 15.8 us: complex_einsum(): jnp.einsum(form, left[0], right[1], precision=HIGHEST)]
    ppermute x8 -> x0, waiting for transfers between devices: 96.9 us -> none  [from_behind(): lax.ppermute(shard, axis, [(i, (i + by) % size) for i in range(size)])]
    all_to_all x10 -> x0, waiting for transfers between devices: 70.5 us -> none  [the longest x2 14 us: likelihood(): lax.all_to_all(spec_re.astype(jnp.bfloat16), ('ty', 'tx'), split_axis=1,...]
    all_to_all x10 -> x0, starting transfers between devices: 53.9 us -> none  [the longest x2 12.6 us: likelihood(): lax.all_to_all(spec_re.astype(jnp.bfloat16), ('ty', 'tx'), split_axis=1,...]
    unnamed x135 -> x1, local copies, waits for them, and re-layouts: 40.8 us -> 1.87 us
    convert_element_type x30 -> x0, local copies, waits for them, and re-layouts: 34.7 us -> none  [the longest x6 10.7 us: patches_of(): shaped.reshape(rows // PATCH, cols // PATCH, PATCH * PATCH)]
    another operation x12 -> x0, local copies, waits for them, and re-layouts: 27.3 us -> none  [the longest x4 16.1 us: attention(): parts = mixed.reshape(number, WIN * WIN, 3, HEADS, D // HEADS)]
  transfers between devices with their start and end apart: 18 -> 0, of which waited for: 18 -> 0; matrix products, arithmetic and copies ran while one was open for 6% -> 0% of each run, Pallas kernels for 0% -> 0%
where the time goes in v1:
time: 174 us; the launch traced here: 173 us
  Pallas kernels  169 us (97%)
  local copies, waits for them, and re-layouts  3.32 us (2%)
    pallas_call x1, Pallas kernels, per_device(): pl.pallas_call(kernel, out_shape=jax.ShapeDtypeStruct(image.shape, F32),...  169 us

profile of v1, /device:TPU:0, one launch (start us, length us, event | category | flops | bytes accessed | tf_op | source)
XLA Modules:
  0.0 172.5 jit_solution(17688409992151694244)
XLA Ops:
  0.0 0.8 reshape.6
  0.8 0.7 reshape.7.keep
  1.5 169.2 %shard_map.235 = f32[256,512]{1,0:T(8,128)} custom-call(s32[2,2]{1,0:T(2,128)} %offsets.1, f32[256,512]{1,0:T(8,128)} %image.1, f32[2,256,512]{2,1,0:T(8,128)} %noise.1, s32[8,64]{1,0:T(8,128)} %reshape.7.keep, f32[2,2,512]{2,1,0:T(2,128)} %norm_gains.1, bf16[512,256]{1,0:T(8,128)(2,1)} %constant.22.clone.w1, bf16[256,512]{1,0:T(8,128)(2,1)} %constant.23.clone.w4, ...), custom_call_target="tpu_custom_call" | custom-call | tf_op jit(solution)/shard_map/pallas_call | solution.py:471
  170.6 1.9 %copy.30 = f32[256,512]{1,0:T(8,128)} copy(f32[256,512]{1,0:T(8,128)} %shard_map.235) | data formatting | bytes 1048576
  (1 shorter events, 0.0 us)
